TPU v7x, 256 devices: a whole 4x4x8 slice. The times are simulated.
256 devices in a mesh: rows: 8 (over y, core), cols: 32 (over z, x).
Axes of the slice: x: 4, y: 4, z: 8, core: 2. Of those that a mesh axis runs over, the one named last changes fastest.
Arguments:
- noise: bfloat16 [32768, 256], P(('rows', 'cols')), may hold values from -24 to 24
- data: bfloat16 [32768, 256], P(('cols', 'rows')), may hold values from -6 to 6
Outputs:
- targets: float32 [32768, 256], P(('rows', 'cols'))
All inputs are finite; a program needn't handle non-finite values.
Results may differ from a plain program's by a relative error of at most 0.00055.
Values may be sent and summed in bfloat16 or wider, within the bound.
A program may use at most 128 MiB of HBM per device.

v0:
```python
import functools
import math

import jax
import jax.numpy as jnp
from jax import lax
from jax.experimental import pallas as pl
from jax.experimental.pallas import tpu as pltpu
from jax.sharding import PartitionSpec as P

MESH = pl.DeviceIdType.MESH
F32 = jnp.float32
BF16 = jnp.bfloat16

ITERS = 4
NR = 8
NZ, NX = 8, 4
NC = NZ * NX
B = 128
D = 256
SPLIT = 48
ROWS = NR * B
CHUNK = 64
SWEEP = 32
GROUP = 8
SHIFT = 20.0
TO_LOG2 = 2.0 / math.log(2.0)
INV_LN2 = 1.0 / math.log(2.0)


def log2(v):
    return jnp.log(v) * INV_LN2


def wait_bytes(ref, sem):
    pltpu.make_async_copy(ref, ref, sem).wait()


def lanes_to_vector(block):
    return jnp.sum(block.T, axis=0, keepdims=True)


def spread(vec):
    return jnp.broadcast_to(vec, (B, B)).T


def kernel(
    noise, data, out,
    tile, dfull, nfull, top, acc, uwide, colw, colv, colc, colm, high8,
    rsrc, rdst, csrc, cmid, cdstx, cdstz, num, pair, numr,
    own_sem, nsem, dsend, drecv, rsem, csem, psem, fsem,
):
    r = lax.axis_index("rows")
    c = lax.axis_index("cols")
    z = c // NX
    x = lax.rem(c, NX)

    def row_peer(k):
        return (lax.rem(r + k, NR), c)

    def x_peer(k):
        return (r, z * NX + lax.rem(x + k, NX))

    def z_peer(k):
        return (r, lax.rem(z + k, NZ) * NX + x)

    own_d = pltpu.make_async_copy(data, dfull.at[c], own_sem.at[0])
    own_d.start()
    own_n = pltpu.make_async_copy(noise, nfull.at[r], own_sem.at[1])
    own_n.start()
    top[...] = jnp.full_like(top, -1e30)
    acc[...] = jnp.zeros_like(acc)

    barrier = pltpu.get_barrier_semaphore()
    peers = [row_peer(k) for k in range(1, NR)]
    peers += [x_peer(k) for k in range(1, NX)] + [z_peer(k) for k in range(1, NZ)]
    for peer in peers:
        pl.semaphore_signal(barrier, inc=1, device_id=peer, device_id_type=MESH)
    own_d.wait()
    own_n.wait()
    pl.semaphore_wait(barrier, len(peers))

    def remote(src, dst, send, recv, peer):
        return pltpu.make_async_remote_copy(
            src_ref=src, dst_ref=dst, send_sem=send, recv_sem=recv, device_id=peer, device_id_type=MESH
        )

    def part(block, h):
        return dfull.at[block, pl.ds(h * SPLIT, SPLIT + h * (B - 2 * SPLIT))]

    def give(block, h, peer):
        remote(part(block, h), part(block, h), dsend, drecv.at[h, block], peer).start()

    def take(block, h):
        wait_bytes(part(block, h), drecv.at[h, block])

    def source(dz, dx):
        return lax.rem(z + dz + NZ, NZ) * NX + lax.rem(x + dx + NX, NX)

    def across(block):
        for k in range(1, NX):
            give(block, 1, x_peer(k))

    for h in (0, 1):
        for k in range(1, NX):
            give(c, h, x_peer(k))
        for k in (2, NZ - 2, 1, NZ - 1):
            give(c, 1 - h, z_peer(k))
    for k in range(1, NR):
        remote(nfull.at[r], nfull.at[r], nsem.at[0], nsem.at[1], row_peer(k)).start()

    def scores(dz, i):
        base = pl.multiple_of(lax.rem(z + dz + NZ, NZ) * NX, NX)
        right = dfull[pl.ds(base, NX)].reshape(NX * B, D)
        left = nfull[pl.ds(2 * i, 2)].reshape(2 * B, D)
        s = lax.dot_general(left, right, (((1,), (1,)), ((), ())), preferred_element_type=F32)
        s = s * (D ** -0.5 * TO_LOG2)
        for k in range(0, 2 * B, CHUNK):
            rows = pl.ds(i * 2 * B + k, CHUNK)
            part = [s[k:k + CHUNK, j * B:(j + 1) * B] for j in range(NX)]
            for j in range(NX):
                tile[base + j, rows, :] = part[j]
            old = top[rows, :]
            new = jnp.maximum(old, jnp.maximum(jnp.maximum(part[0], part[1]), jnp.maximum(part[2], part[3])))
            total = acc[rows, :] * jnp.exp2(old - new)
            for j in range(NX):
                total = total + jnp.exp2(part[j] - new)
            top[rows, :] = new
            acc[rows, :] = total

    ready = []

    def work(count):
        for _ in range(min(count, len(ready))):
            ready.pop(0)()

    def add_set(dz):
        def rest():
            for dx in range(1, NX):
                take(source(dz, -dx), 1)
            scores(dz, 0)

        ready.append(rest)
        for i in range(1, NR // 2):
            ready.append(functools.partial(scores, dz, i))

    half = NZ // 2
    others = (1, 3, 2)

    def far(h, turn):
        for sign in (-1, 1):
            block = source(2 * sign, 0)
            take(block, h)
            if sign == turn:
                give(block, h, z_peer((NZ - 2 * sign) % NZ))
            give(block, h, z_peer((NZ - sign) % NZ))
            if h:
                across(block)

    def along(d):
        for dx in others:
            for sign in (-1, 1):
                block = source(d * sign, -dx)
                take(block, 0)
                if d < half - 1 or (dx != 2) == (sign < 0):
                    give(block, 0, z_peer((NZ - sign) % NZ))
                work(1)

    def spread_second(d):
        for sign in (-1, 1)[:2 if d < half else 1]:
            block = source(d * sign, 0)
            take(block, 1)
            across(block)
            work(1)

    for dx in others:
        block = source(0, -dx)
        take(block, 0)
        give(block, 0, z_peer(1))
        give(block, 0, z_peer(NZ - 1))
    spread_second(1)
    far(1, 1)
    far(0, -1)
    along(1)
    wait_bytes(nfull.at[pl.ds(0, NR - 1)], nsem.at[1])
    add_set(0)
    for sign in (-1, 1):
        take(source(sign, 0), 0)
        add_set(sign)
    spread_second(3)
    along(2)
    spread_second(half)
    add_set(-2)
    add_set(2)
    along(3)
    for sign in (-1, 1):
        take(source(3 * sign, 0), 0)
        add_set(3 * sign)
    work(8)
    for dx in range(NX):
        take(source(half, -dx), 0)
        work(1)
    add_set(half)
    work(len(ready))
    wait_bytes(dfull.at[pl.ds(0, NC - 1)], dsend)
    wait_bytes(nfull.at[pl.ds(0, NR - 1)], nsem.at[0])

    def send_all(src, dst, sems, group, size):
        for k in sorted(range(1, size), key=lambda k: abs(k - size // 2)):
            remote(src, dst.at[k - 1], sems.at[0], sems.at[1], group(k)).start()

    def lse(own, others, n):
        high = own
        for k in range(n):
            high = jnp.maximum(high, others[k])
        total = jnp.exp2(own - high)
        for k in range(n):
            total = total + jnp.exp2(others[k] - high)
        return high + log2(total)

    def add(own, others, n):
        for k in range(n):
            own = own + others[k]
        return own

    def rows_out(t, h):
        send_all(rsrc.at[t, h], rdst.at[t, h], rsem.at[t, h], row_peer, NR)

    def rows_in(t, h, combine):
        dst = rdst.at[t, h]
        wait_bytes(dst, rsem.at[t, h, 1])
        wait_bytes(dst, rsem.at[t, h, 0])
        return combine(rsrc[t, h], dst, NR - 1)

    def over_cols(t, combine):
        send_all(csrc.at[t, 1], cdstz.at[t, 0], csem.at[t, 1], z_peer, NZ)
        send_all(csrc.at[t, 0], cdstx.at[t, 0], csem.at[t, 0], x_peer, NX)
        wait_bytes(cdstx.at[t, 0], csem.at[t, 0, 1])
        cmid[t, 0] = combine(csrc[t, 0], cdstx.at[t, 0], NX - 1)
        send_all(cmid.at[t, 0], cdstz.at[t, 1], csem.at[t, 2], z_peer, NZ)
        wait_bytes(cdstz.at[t, 0], csem.at[t, 1, 1])
        cmid[t, 1] = combine(csrc[t, 1], cdstz.at[t, 0], NZ - 1)
        send_all(cmid.at[t, 1], cdstx.at[t, 1], csem.at[t, 3], x_peer, NX)
        wait_bytes(cdstz.at[t, 1], csem.at[t, 2, 1])
        first = combine(cmid[t, 0], cdstz.at[t, 1], NZ - 1)
        wait_bytes(cdstx.at[t, 1], csem.at[t, 3, 1])
        second = combine(cmid[t, 1], cdstx.at[t, 1], NX - 1)
        wait_bytes(cdstx.at[t, 0], csem.at[t, 0, 0])
        wait_bytes(cdstz.at[t, 0], csem.at[t, 1, 0])
        wait_bytes(cdstz.at[t, 1], csem.at[t, 2, 0])
        wait_bytes(cdstx.at[t, 1], csem.at[t, 3, 0])
        return first, second

    hr = NR // 2
    for h in range(2):
        for b in range(hr):
            rows = pl.ds((h * hr + b) * B, B)
            high = top[rows, :].T
            row_top = jnp.max(high, axis=0, keepdims=True)
            total = jnp.sum(acc[rows, :].T * jnp.exp2(high - row_top), axis=0, keepdims=True)
            rsrc[0, h, b:b + 1, :] = row_top + log2(total)
        rows_out(0, h)

    def widen(h, values):
        for b in range(hr):
            uwide[pl.ds((h * hr + b) * B, B), :] = spread(values[b:b + 1, :])


    fold = (SWEEP // 8, 8, B)
    steps = ROWS // SWEEP // 2
    zeros = (jnp.zeros((8, B), F32),) * NC

    def top_step(i, highs):
        rows = pl.ds(pl.multiple_of(i * SWEEP, SWEEP), SWEEP)
        u = uwide[rows, :]
        return tuple(
            jnp.maximum(high, jnp.max((tile[j, rows, :] + u).reshape(fold), axis=0)) for j, high in enumerate(highs)
        )

    highs = (jnp.full((8, B), -1e30, F32),) * NC
    for h in range(2):
        widen(h, -rows_in(0, h, lse))
        highs = lax.fori_loop(h * steps, (h + 1) * steps, top_step, highs)
    for j in range(NC):
        high = jnp.max(highs[j], axis=0, keepdims=True)
        colm[j:j + 1, :] = high
        high8[j] = jnp.broadcast_to(high - SHIFT, (8, B))

    def exp_step(i, totals):
        rows = pl.ds(pl.multiple_of(i * SWEEP, SWEEP), SWEEP)
        u = uwide[rows, :].reshape(fold)
        sums = []
        for j in range(NC):
            e = jnp.exp2(tile[j, rows, :].reshape(fold) + (u - high8[j]))
            tile[j, rows, :] = e.reshape(SWEEP, B)
            sums.append(totals[j] + jnp.sum(e, axis=0))
        return tuple(sums)

    totals = lax.fori_loop(0, ROWS // SWEEP, exp_step, zeros)
    for j in range(NC):
        colc[j:j + 1, :] = jnp.sum(totals[j], axis=0, keepdims=True)
    hc = NC // 2
    csrc[0] = (colm[...] + (log2(colc[...]) - SHIFT)).reshape(2, hc, B)
    for h, logs in enumerate(over_cols(0, lse)):
        half = pl.ds(h * hc, hc)
        colw[half, :] = jnp.exp2(colm[half, :] - logs + SHIFT)
        colv[half, :] = colw[half, :]

    def iteration(t, carry):
        def rows_pass(i, carry):
            rows = pl.ds(pl.multiple_of(i * 2 * B, 2 * B), 2 * B)
            total = tile[0, rows, :] * colv[0:1, :]
            for j in range(1, NC):
                total = total + tile[j, rows, :] * colv[j:j + 1, :]
            acc[rows, :] = total
            return carry

        for h in range(2):
            lax.fori_loop(h * hr // 2, (h + 1) * hr // 2, rows_pass, 0)
            for b in range(hr):
                rsrc[t, h, b:b + 1, :] = lanes_to_vector(acc[pl.ds((h * hr + b) * B, B), :])
            rows_out(t, h)

        def step(i, totals):
            rows = pl.ds(pl.multiple_of(i * SWEEP, SWEEP), SWEEP)
            u = uwide[rows, :]
            return tuple(
                total + jnp.sum((tile[j, rows, :] * u).reshape(fold), axis=0) for j, total in enumerate(totals)
            )

        totals = zeros
        for h in range(2):
            widen(h, 1.0 / rows_in(t, h, add))
            totals = lax.fori_loop(h * steps, (h + 1) * steps, step, totals)
        for j in range(NC):
            colc[j:j + 1, :] = jnp.sum(totals[j], axis=0, keepdims=True)
        csrc[t] = (colc[...] * colw[...]).reshape(2, hc, B)
        for h, sums in enumerate(over_cols(t, add)):
            half = pl.ds(h * hc, hc)
            colv[half, :] = colw[half, :] / sums
        return carry

    lax.fori_loop(1, ITERS, iteration, 0)

    y = r // 2
    core = lax.rem(r, 2)
    partner = (2 * y + 1 - core, c)

    def target(i):
        return lax.rem(y + 6 - i + 3 * (i // 2) + 2 * (i // 3), NR // 2)

    def weigh(i):
        q = target(i)
        rows = pl.ds(pl.multiple_of(q * 2 * B, 2 * B), 2 * B)
        n = total = None
        for g in range(0, NC, GROUP):
            parts = []
            for j in range(g, g + GROUP):
                w = (tile[j, rows, :] * colv[j:j + 1, :]).astype(BF16)
                parts.append(w)
                wide = w.astype(F32)
                total = wide if total is None else total + wide
            part = jnp.dot(
                jnp.concatenate(parts, axis=1),
                dfull[pl.ds(g, GROUP)].reshape(GROUP * B, D),
                preferred_element_type=F32,
            )
            n = part if n is None else n + part
        for h in range(2):
            num[i, h, 0:B] = n[h * B:(h + 1) * B]
            sums = lanes_to_vector(total[h * B:(h + 1) * B])
            num[i, h, B:B + 8, 0:B] = jnp.broadcast_to(sums, (8, B))
            num[i, h, B:B + 8, B:D] = jnp.zeros((8, B), F32)
        remote(num.at[i, 1 - core], pair.at[i], psem.at[0, i], psem.at[1, i], partner).start()

    def join(i):
        wait_bytes(pair.at[i], psem.at[1, i])
        num[i, core] = num[i, core] + pair[i]

    def hand_over(i):
        join(i)
        q = target(i)
        remote(num.at[i, core], numr.at[i], fsem.at[0], fsem.at[1], (2 * q + core, c)).start()

    weigh(0)

    def final(i, carry):
        weigh(i)
        hand_over(i - 1)
        return carry

    last = NR // 2 - 1
    lax.fori_loop(1, last + 1, final, 0)
    join(last)
    wait_bytes(numr, fsem.at[1])
    total = num[last, core]
    for k in range(last):
        total = total + numr[k]
    scale = spread(total[B:B + 1, 0:B])
    out[:, 0:B] = total[0:B, 0:B] / scale
    out[:, B:D] = total[0:B, B:D] / scale
    wait_bytes(numr, fsem.at[0])
    for i in range(last + 1):
        wait_bytes(pair.at[i], psem.at[0, i])


def solution(mesh):
    vmem, dma = pltpu.VMEM, pltpu.SemaphoreType.DMA
    scratch = [
        vmem((NC, ROWS, B), F32),
        vmem((NC, B, D), BF16),
        vmem((NR, B, D), BF16),
        vmem((ROWS, B), F32),
        vmem((ROWS, B), F32),
        vmem((ROWS, B), F32),
        vmem((NC, B), F32),
        vmem((NC, B), F32),
        vmem((NC, B), F32),
        vmem((NC, B), F32),
        vmem((NC, 8, B), F32),
        vmem((ITERS, 2, NR // 2, B), F32),
        vmem((ITERS, 2, NR - 1, NR // 2, B), F32),
        vmem((ITERS, 2, NC // 2, B), F32),
        vmem((ITERS, 2, NC // 2, B), F32),
        vmem((ITERS, 2, NX - 1, NC // 2, B), F32),
        vmem((ITERS, 2, NZ - 1, NC // 2, B), F32),
        vmem((NR // 2, 2, B + 8, D), F32),
        vmem((NR // 2, B + 8, D), F32),
        vmem((NR // 2 - 1, B + 8, D), F32),
        dma((2,)),
        dma((2,)),
        dma,
        dma((2, NC)),
        dma((ITERS, 2, 2)),
        dma((ITERS, 4, 2)),
        dma((2, NR // 2)),
        dma((2,)),
    ]

    def per_device(noise, data):
        return pl.pallas_call(
            kernel,
            out_shape=jax.ShapeDtypeStruct((B, D), F32),
            in_specs=[pl.BlockSpec(memory_space=pl.ANY)] * 2,
            out_specs=pl.BlockSpec(memory_space=pltpu.VMEM),
            scratch_shapes=scratch,
            compiler_params=pltpu.CompilerParams(
                collective_id=0, has_side_effects=True, vmem_limit_bytes=40 << 20
            ),
        )(noise, data)

    return jax.shard_map(
        per_device,
        mesh=mesh,
        in_specs=(P(("rows", "cols"), None), P(("cols", "rows"), None)),
        out_specs=P(("rows", "cols"), None),
        check_vma=False,
    )
```

profile of v0, /device:TPU:1, one launch (start us, length us, event | category | flops | bytes accessed | tf_op | source)
XLA Modules:
  0.0 105.4 jit_solution(1828248113604574890)
XLA Ops:
  0.0 0.0 copy-start
  0.0 0.8 copy-done
  0.8 0.0 copy-start.1
  0.8 0.8 copy-done.1
  1.7 103.0 %shard_map.28 = f32[128,256]{1,0:T(8,128)S(1)} custom-call(bf16[128,256]{1,0:T(8,128)(2,1)S(1)} %copy-done, bf16[128,256]{1,0:T(8,128)(2,1)S(1)} %copy-done.1), custom_call_target="tpu_custom_call" | custom-call | tf_op jit(solution)/shard_map/pallas_call | solution.py:441
  104.7 0.7 copy.4
Async XLA Ops:
  0.0 0.8 copy-start
  0.8 0.8 copy-start.1
where the time goes:
time: 106 us; the launch traced here: 105 us
  Pallas kernels  103 us (97%)
  local copies, waits for them, and re-layouts  2.34 us (2%)
    pallas_call x1, Pallas kernels, per_device(): pl.pallas_call(kernel, out_shape=jax.ShapeDtypeStruct((B, D), F32), in_sp...  103 us
    unnamed x5, local copies, waits for them, and re-layouts  2.34 us

commit v1 on v0

--- a/solution.py
+++ b/solution.py
@@ -382,15 +382,16 @@
         q = target(i)
         remote(num.at[i, core], numr.at[i], fsem.at[0], fsem.at[1], (2 * q + core, c)).start()
 
-    weigh(0)
-
-    def final(i, carry):
+    def first(i, carry):
         weigh(i)
-        hand_over(i - 1)
         return carry
 
     last = NR // 2 - 1
-    lax.fori_loop(1, last + 1, final, 0)
+    lax.fori_loop(0, last, first, 0)
+    hand_over(0)
+    hand_over(1)
+    weigh(last)
+    hand_over(2)
     join(last)
     wait_bytes(numr, fsem.at[1])
     total = num[last, core]

time: 106 us -> 105 us (level)
  no operation moved by 1% of the time
where the time goes in v1:
time: 105 us
  Pallas kernels  103 us (98%)
  local copies, waits for them, and re-layouts  2.34 us (2%)
    pallas_call x1, Pallas kernels, per_device(): pl.pallas_call(kernel, out_shape=jax.ShapeDtypeStruct((B, D), F32), in_sp...  103 us
    unnamed x5, local copies, waits for them, and re-layouts  2.34 us

profile of v1, /device:TPU:1, one launch (start us, length us, event | category | flops | bytes accessed | tf_op | source)
XLA Modules:
  0.0 105.0 jit_solution(17661799360102427580)
XLA Ops:
  0.0 0.0 copy-start
  0.0 0.8 copy-done
  0.8 0.0 copy-start.1
  0.8 0.8 copy-done.1
  1.7 102.6 %shard_map.28 = f32[128,256]{1,0:T(8,128)S(1)} custom-call(bf16[128,256]{1,0:T(8,128)(2,1)S(1)} %copy-done, bf16[128,256]{1,0:T(8,128)(2,1)S(1)} %copy-done.1), custom_call_target="tpu_custom_call" | custom-call | tf_op jit(solution)/shard_map/pallas_call | solution.py:442
  104.3 0.7 copy.4
Async XLA Ops:
  0.0 0.8 copy-start
  0.8 0.8 copy-start.1

commit v2 on v1

--- a/solution.py
+++ b/solution.py
@@ -202,8 +202,6 @@
         work(1)
     add_set(half)
     work(len(ready))
-    wait_bytes(dfull.at[pl.ds(0, NC - 1)], dsend)
-    wait_bytes(nfull.at[pl.ds(0, NR - 1)], nsem.at[0])
 
     def send_all(src, dst, sems, group, size):
         for k in sorted(range(1, size), key=lambda k: abs(k - size // 2)):
@@ -229,12 +227,11 @@
     def rows_in(t, h, combine):
         dst = rdst.at[t, h]
         wait_bytes(dst, rsem.at[t, h, 1])
-        wait_bytes(dst, rsem.at[t, h, 0])
         return combine(rsrc[t, h], dst, NR - 1)
 
     def over_cols(t, combine):
+        send_all(csrc.at[t, 0], cdstx.at[t, 0], csem.at[t, 0], x_peer, NX)
         send_all(csrc.at[t, 1], cdstz.at[t, 0], csem.at[t, 1], z_peer, NZ)
-        send_all(csrc.at[t, 0], cdstx.at[t, 0], csem.at[t, 0], x_peer, NX)
         wait_bytes(cdstx.at[t, 0], csem.at[t, 0, 1])
         cmid[t, 0] = combine(csrc[t, 0], cdstx.at[t, 0], NX - 1)
         send_all(cmid.at[t, 0], cdstz.at[t, 1], csem.at[t, 2], z_peer, NZ)
@@ -245,10 +242,6 @@
         first = combine(cmid[t, 0], cdstz.at[t, 1], NZ - 1)
         wait_bytes(cdstx.at[t, 1], csem.at[t, 3, 1])
         second = combine(cmid[t, 1], cdstx.at[t, 1], NX - 1)
-        wait_bytes(cdstx.at[t, 0], csem.at[t, 0, 0])
-        wait_bytes(cdstz.at[t, 0], csem.at[t, 1, 0])
-        wait_bytes(cdstz.at[t, 1], csem.at[t, 2, 0])
-        wait_bytes(cdstx.at[t, 1], csem.at[t, 3, 0])
         return first, second
 
     hr = NR // 2
@@ -393,6 +386,17 @@
     weigh(last)
     hand_over(2)
     join(last)
+
+    wait_bytes(dfull.at[pl.ds(0, NC - 1)], dsend)
+    wait_bytes(nfull.at[pl.ds(0, NR - 1)], nsem.at[0])
+    for t in range(ITERS):
+        for h in range(2):
+            wait_bytes(rdst.at[t, h], rsem.at[t, h, 0])
+        wait_bytes(cdstx.at[t, 0], csem.at[t, 0, 0])
+        wait_bytes(cdstz.at[t, 0], csem.at[t, 1, 0])
+        wait_bytes(cdstz.at[t, 1], csem.at[t, 2, 0])
+        wait_bytes(cdstx.at[t, 1], csem.at[t, 3, 0])
+
     wait_bytes(numr, fsem.at[1])
     total = num[last, core]
     for k in range(last):

time: 105 us -> 105 us (level)
  no operation moved by 1% of the time
where the time goes in v2:
time: 105 us
  Pallas kernels  102 us (97%)
  local copies, waits for them, and re-layouts  2.34 us (2%)
    pallas_call x1, Pallas kernels, per_device(): pl.pallas_call(kernel, out_shape=jax.ShapeDtypeStruct((B, D), F32), in_sp...  102 us
    unnamed x5, local copies, waits for them, and re-layouts  2.34 us

profile of v2, /device:TPU:1, one launch (start us, length us, event | category | flops | bytes accessed | tf_op | source)
XLA Modules:
  0.0 104.7 jit_solution(2617859436941584340)
XLA Ops:
  0.0 0.0 copy-start
  0.0 0.8 copy-done
  0.8 0.0 copy-start.1
  0.8 0.8 copy-done.1
  1.7 102.4 %shard_map.28 = f32[128,256]{1,0:T(8,128)S(1)} custom-call(bf16[128,256]{1,0:T(8,128)(2,1)S(1)} %copy-done, bf16[128,256]{1,0:T(8,128)(2,1)S(1)} %copy-done.1), custom_call_target="tpu_custom_call" | custom-call | tf_op jit(solution)/shard_map/pallas_call | solution.py:446
  104.1 0.7 copy.4
Async XLA Ops:
  0.0 0.8 copy-start
  0.8 0.8 copy-start.1
